TPU v7x, 32 devices: a whole 2x2x4 slice. The times are simulated.
32 devices in a mesh: mod: 2 (over x), dp: 16 (over z, y, core).
Axes of the slice: x: 2, y: 2, z: 4, core: 2. Of those that a mesh axis runs over, the one named last changes fastest.
Arguments:
- text: bfloat16 [128, 40, 768], P(('mod', 'dp')), may hold values from -6 to 6
- lengths: int32 [128], P(('mod', 'dp')), may hold values from 8 to 40, as said below
- patches: bfloat16 [128, 145, 1024], P(('mod', 'dp')), may hold values from -6 to 6
- w_query: bfloat16 [768, 768], P(('mod', 'dp')), may hold values from -0.21875 to 0.21875
- w_key: bfloat16 [768, 768], P(('mod', 'dp')), may hold values from -0.21875 to 0.21875
- w_value: bfloat16 [768, 768], P(('mod', 'dp')), may hold values from -0.21875 to 0.21875
- w_out: bfloat16 [768, 768], P(('mod', 'dp')), may hold values from -0.625 to 0.625
- b_query: float32 [768], replicated, may hold values from -3 to 3
- b_value: float32 [768], replicated, may hold values from -3 to 3
- b_out: float32 [768], replicated, may hold values from -3 to 3
- gain_one: float32 [768], replicated, may hold values from 0.5 to 1.5
- bias_one: float32 [768], replicated, may hold values from -3 to 3
- w_image: bfloat16 [1024, 768], P(('mod', 'dp')), may hold values from -0.1875 to 0.1875
- b_image: float32 [768], replicated, may hold values from -3 to 3
- c_query: bfloat16 [768, 768], P(('mod', 'dp')), may hold values from -0.21875 to 0.21875
- c_key: bfloat16 [768, 768], P(('mod', 'dp')), may hold values from -0.21875 to 0.21875
- c_value: bfloat16 [768, 768], P(('mod', 'dp')), may hold values from -0.21875 to 0.21875
- c_out: bfloat16 [768, 768], P(('mod', 'dp')), may hold values from -0.875 to 0.875
- cb_query: float32 [768], replicated, may hold values from -3 to 3
- cb_value: float32 [768], replicated, may hold values from -3 to 3
- cb_out: float32 [768], replicated, may hold values from -3 to 3
- gain_two: float32 [768], replicated, may hold values from 0.5 to 1.5
- bias_two: float32 [768], replicated, may hold values from -3 to 3
- w_inner: bfloat16 [768, 3072], P(('mod', 'dp')), may hold values from -0.21875 to 0.21875
- b_inner: float32 [3072], replicated, may hold values from -3 to 3
- w_outer: bfloat16 [3072, 768], P(('mod', 'dp')), may hold values from -0.21875 to 0.21875
- b_outer: float32 [768], replicated, may hold values from -3 to 3
- gain_three: float32 [768], replicated, may hold values from 0.5 to 1.5
- bias_three: float32 [768], replicated, may hold values from -3 to 3
- cotangent: bfloat16 [128, 40, 768], P(('mod', 'dp')), may hold values from -6 to 6
Outputs:
- mixed_out: float32 [128, 40, 768], P(('mod', 'dp'))
- grad_text: float32 [128, 40, 768], P(('mod', 'dp'))
- grad_patches: float32 [128, 145, 1024], P(('mod', 'dp'))
- grad_w_query: float32 [768, 768], P(('mod', 'dp'))
- grad_w_key: float32 [768, 768], P(('mod', 'dp'))
- grad_w_value: float32 [768, 768], P(('mod', 'dp'))
- grad_w_out: float32 [768, 768], P(('mod', 'dp'))
- grad_b_query: float32 [768], replicated
- grad_b_value: float32 [768], replicated
- grad_b_out: float32 [768], replicated
- grad_gain_one: float32 [768], replicated
- grad_bias_one: float32 [768], replicated
- grad_w_image: float32 [1024, 768], P(('mod', 'dp'))
- grad_b_image: float32 [768], replicated
- grad_c_query: float32 [768, 768], P(('mod', 'dp'))
- grad_c_key: float32 [768, 768], P(('mod', 'dp'))
- grad_c_value: float32 [768, 768], P(('mod', 'dp'))
- grad_c_out: float32 [768, 768], P(('mod', 'dp'))
- grad_cb_query: float32 [768], replicated
- grad_cb_value: float32 [768], replicated
- grad_cb_out: float32 [768], replicated
- grad_gain_two: float32 [768], replicated
- grad_bias_two: float32 [768], replicated
- grad_w_inner: float32 [768, 3072], P(('mod', 'dp'))
- grad_b_inner: float32 [3072], replicated
- grad_w_outer: float32 [3072, 768], P(('mod', 'dp'))
- grad_b_outer: float32 [768], replicated
- grad_gain_three: float32 [768], replicated
- grad_bias_three: float32 [768], replicated
Inputs may be any that keep to these rules, and one draw needn't show every extreme that they name: `lengths`: real tokens of each item; some item has exactly 40 and some exactly 8.
All inputs are finite; a program needn't handle non-finite values.
Results may differ from a plain program's by a relative error of at most 0.025.
Values may be sent and summed in bfloat16 or wider, within the bound.
No kernel may reach another device: no remote copies, remote signals or barrier semaphores. Data moves between devices by JAX's collectives and lax.ppermute only.
A program may use at most 192 MiB of HBM per device.

v0:
```python
from functools import partial

import jax
import jax.numpy as jnp
from jax import lax
from jax.sharding import PartitionSpec as P

D = 768
HEADS = 12
HEAD_DIM = 64
VW = 1024
NP = 145
SEQ = 40
ITEMS_DEV = 4


neg_large = -1000000000.0
ln_eps = 1e-06


def swapped(block, axis, apart):
    count = lax.axis_size(axis)
    route = []
    for low in range(count):
        high = low | 1 << apart
        if high != low and high < count:
            route += [(low, high), (high, low)]
    return lax.ppermute(block, axis, route)


def layer_norm(values, gain_vec, shift_vec):
    centered = values - jnp.mean(values, axis=-1, keepdims=True)
    spread = jnp.mean(centered * centered, axis=-1, keepdims=True)
    return centered * lax.rsqrt(spread + ln_eps) * gain_vec + shift_vec


def project(left_rows, weight):
    return jnp.dot(left_rows, weight, preferred_element_type=jnp.float32)


def project_back(grad_rows, weight):
    return lax.dot_general(
        grad_rows, weight, (((1,), (1,)), ((), ())), preferred_element_type=jnp.float32
    )


def weight_grad(left_rows, grad_rows):
    return lax.dot_general(
        left_rows, grad_rows, (((0,), (0,)), ((), ())), preferred_element_type=jnp.float32
    )


def row_total(grad_rows):
    return jnp.sum(grad_rows.astype(jnp.float32), axis=0)


def split_heads(values):
    return values.reshape(ITEMS_DEV, -1, HEADS, HEAD_DIM)


def attend_forward(query_rows, key_rows, value_rows, mask_bias):
    scores = (
        jnp.einsum(
            "bqhe,bkhe->bhqk",
            split_heads(query_rows),
            split_heads(key_rows),
            preferred_element_type=jnp.float32,
        )
        * HEAD_DIM ** (-0.5)
        + mask_bias
    )
    row_top = jnp.max(scores, axis=-1, keepdims=True)
    weights = jnp.exp(scores - row_top)
    probs_full = weights / jnp.sum(weights, axis=-1, keepdims=True)
    probs_low = probs_full.astype(jnp.bfloat16)
    heads_out = jnp.einsum(
        "bhqk,bkhe->bqhe", probs_low, split_heads(value_rows), preferred_element_type=jnp.float32
    )
    return (heads_out.reshape(-1, D).astype(jnp.bfloat16), probs_full, probs_low)


def attend_backward(grad_rows, query_rows, key_rows, value_rows, probs_full, probs_low):
    grad_split = split_heads(grad_rows)
    grad_probs = jnp.einsum(
        "bqhe,bkhe->bhqk", grad_split, split_heads(value_rows), preferred_element_type=jnp.float32
    )
    grad_scores = probs_full * (
        grad_probs - jnp.sum(probs_full * grad_probs, axis=-1, keepdims=True)
    )
    grad_scores = grad_scores.astype(jnp.bfloat16)
    score_scale = HEAD_DIM ** (-0.5)
    grad_query = (
        jnp.einsum(
            "bhqk,bkhe->bqhe",
            grad_scores,
            split_heads(key_rows),
            preferred_element_type=jnp.float32,
        )
        * score_scale
    )
    grad_keys = (
        jnp.einsum(
            "bhqk,bqhe->bkhe",
            grad_scores,
            split_heads(query_rows),
            preferred_element_type=jnp.float32,
        )
        * score_scale
    )
    grad_values = jnp.einsum(
        "bhqk,bqhe->bkhe", probs_low, grad_split, preferred_element_type=jnp.float32
    )
    return (
        grad_query.reshape(-1, D).astype(jnp.bfloat16),
        grad_keys.reshape(-1, D).astype(jnp.bfloat16),
        grad_values.reshape(-1, D).astype(jnp.bfloat16),
    )


def local(
    text,
    lengths,
    patches,
    w_query,
    w_key,
    w_value,
    w_out,
    b_query,
    b_value,
    b_out,
    gain_one,
    bias_one,
    w_image,
    b_image,
    c_query,
    c_key,
    c_value,
    c_out,
    cb_query,
    cb_value,
    cb_out,
    gain_two,
    bias_two,
    w_inner,
    b_inner,
    w_outer,
    b_outer,
    gain_three,
    bias_three,
    cotangent,
):
    w_query, w_key, w_value, w_out, w_image, c_query, c_key, c_value, c_out = (
        lax.all_gather(w_query, ("mod", "dp"), axis=0, tiled=True),
        lax.all_gather(w_key, ("mod", "dp"), axis=0, tiled=True),
        lax.all_gather(w_value, ("mod", "dp"), axis=0, tiled=True),
        lax.all_gather(w_out, ("mod", "dp"), axis=0, tiled=True),
        lax.all_gather(w_image, ("mod", "dp"), axis=0, tiled=True),
        lax.all_gather(c_query, ("mod", "dp"), axis=0, tiled=True),
        lax.all_gather(c_key, ("mod", "dp"), axis=0, tiled=True),
        lax.all_gather(c_value, ("mod", "dp"), axis=0, tiled=True),
        lax.all_gather(c_out, ("mod", "dp"), axis=0, tiled=True),
    )
    positions = lax.broadcasted_iota(jnp.int32, (ITEMS_DEV, SEQ), 1)
    keep_mask = (positions < lengths[:, None]).astype(jnp.float32)
    mask_bias = jnp.where(keep_mask > 0.5, 0.0, neg_large)[:, None, None, :]
    text_rows = text.reshape(-1, D)
    query_rows = (project(text_rows, w_query) + b_query).astype(jnp.bfloat16)
    key_rows = project(text_rows, w_key).astype(jnp.bfloat16)
    value_rows = (project(text_rows, w_value) + b_value).astype(jnp.bfloat16)
    attn_rows, self_full, self_low = attend_forward(query_rows, key_rows, value_rows, mask_bias)
    branch = project(attn_rows, w_out) + b_out
    hidden_full, norm_one_back = jax.vjp(
        layer_norm, text_rows.astype(jnp.float32) + branch, gain_one, bias_one
    )
    hidden = hidden_full.astype(jnp.bfloat16)
    cross_query = (project(hidden, c_query) + cb_query).astype(jnp.bfloat16)
    image_source = patches.reshape(-1, VW)
    image_rows = (project(image_source, w_image) + b_image).astype(jnp.bfloat16)
    own_keys = project(image_rows, c_key).astype(jnp.bfloat16)
    own_values = (project(image_rows, c_value) + cb_value).astype(jnp.bfloat16)
    cross_keys, cross_values = swapped((own_keys, own_values), "mod", 0)
    w_inner, w_outer = (
        lax.all_gather(w_inner, ("mod", "dp"), axis=0, tiled=True),
        lax.all_gather(w_outer, ("mod", "dp"), axis=0, tiled=True),
    )
    cross_rows, cross_full, cross_low = attend_forward(cross_query, cross_keys, cross_values, 0.0)
    cross_branch = project(cross_rows, c_out) + cb_out
    joint_full, norm_two_back = jax.vjp(
        layer_norm, hidden.astype(jnp.float32) + cross_branch, gain_two, bias_two
    )
    joint_rows = joint_full.astype(jnp.bfloat16)
    inner_pre = project(joint_rows, w_inner) + b_inner
    active_full, gelu_back = jax.vjp(partial(jax.nn.gelu, approximate=False), inner_pre)
    active = active_full.astype(jnp.bfloat16)
    outer_pre = project(active, w_outer) + b_outer
    result_full, norm_three_back = jax.vjp(
        layer_norm, joint_rows.astype(jnp.float32) + outer_pre, gain_three, bias_three
    )
    mixed_out = result_full.reshape(ITEMS_DEV, SEQ, D) * keep_mask[:, :, None]
    grad_result = (cotangent.astype(jnp.float32) * keep_mask[:, :, None]).reshape(-1, D)
    grad_sum_three, grad_gain_three, grad_bias_three = norm_three_back(grad_result)
    grad_outer = grad_sum_three.astype(jnp.bfloat16)
    grad_w_outer = weight_grad(active, grad_outer)
    grad_b_outer = row_total(grad_outer)
    (grad_inner_full,) = gelu_back(project_back(grad_outer, w_outer))
    grad_inner = grad_inner_full.astype(jnp.bfloat16)
    grad_w_inner = weight_grad(joint_rows, grad_inner)
    grad_b_inner = row_total(grad_inner)
    grad_joint = grad_sum_three + project_back(grad_inner, w_inner)
    grad_w_inner, grad_w_outer = (
        lax.psum_scatter(grad_w_inner, ("mod", "dp"), scatter_dimension=0, tiled=True),
        lax.psum_scatter(grad_w_outer, ("mod", "dp"), scatter_dimension=0, tiled=True),
    )
    grad_sum_two, grad_gain_two, grad_bias_two = norm_two_back(grad_joint)
    grad_cross_branch = grad_sum_two.astype(jnp.bfloat16)
    grad_c_out = weight_grad(cross_rows, grad_cross_branch)
    grad_cb_out = row_total(grad_cross_branch)
    grad_cross_rows = project_back(grad_cross_branch, c_out).astype(jnp.bfloat16)
    grad_cross_query, grad_cross_keys, grad_cross_values = attend_backward(
        grad_cross_rows, cross_query, cross_keys, cross_values, cross_full, cross_low
    )
    grad_c_query = weight_grad(hidden, grad_cross_query)
    grad_cb_query = row_total(grad_cross_query)
    grad_hidden = grad_sum_two + project_back(grad_cross_query, c_query)
    back_keys, back_values = swapped((grad_cross_keys, grad_cross_values), "mod", 0)
    grad_c_key = weight_grad(image_rows, back_keys)
    grad_c_value = weight_grad(image_rows, back_values)
    grad_cb_value = row_total(back_values)
    grad_image = (project_back(back_keys, c_key) + project_back(back_values, c_value)).astype(
        jnp.bfloat16
    )
    grad_w_image = weight_grad(image_source, grad_image)
    grad_b_image = row_total(grad_image)
    grad_patches = project_back(grad_image, w_image)
    grad_sum_one, grad_gain_one, grad_bias_one = norm_one_back(grad_hidden)
    grad_branch = grad_sum_one.astype(jnp.bfloat16)
    grad_w_out = weight_grad(attn_rows, grad_branch)
    grad_b_out = row_total(grad_branch)
    grad_attn = project_back(grad_branch, w_out).astype(jnp.bfloat16)
    grad_query, grad_keys, grad_values = attend_backward(
        grad_attn, query_rows, key_rows, value_rows, self_full, self_low
    )
    grad_w_query = weight_grad(text_rows, grad_query)
    grad_w_key = weight_grad(text_rows, grad_keys)
    grad_w_value = weight_grad(text_rows, grad_values)
    grad_b_query = row_total(grad_query)
    grad_b_value = row_total(grad_values)
    grad_text = (
        grad_sum_one
        + project_back(grad_query, w_query)
        + project_back(grad_keys, w_key)
        + project_back(grad_values, w_value)
    )
    (
        grad_w_query,
        grad_w_key,
        grad_w_value,
        grad_w_out,
        grad_w_image,
        grad_c_query,
        grad_c_key,
        grad_c_value,
        grad_c_out,
    ) = (
        lax.psum_scatter(grad_w_query, ("mod", "dp"), scatter_dimension=0, tiled=True),
        lax.psum_scatter(grad_w_key, ("mod", "dp"), scatter_dimension=0, tiled=True),
        lax.psum_scatter(grad_w_value, ("mod", "dp"), scatter_dimension=0, tiled=True),
        lax.psum_scatter(grad_w_out, ("mod", "dp"), scatter_dimension=0, tiled=True),
        lax.psum_scatter(grad_w_image, ("mod", "dp"), scatter_dimension=0, tiled=True),
        lax.psum_scatter(grad_c_query, ("mod", "dp"), scatter_dimension=0, tiled=True),
        lax.psum_scatter(grad_c_key, ("mod", "dp"), scatter_dimension=0, tiled=True),
        lax.psum_scatter(grad_c_value, ("mod", "dp"), scatter_dimension=0, tiled=True),
        lax.psum_scatter(grad_c_out, ("mod", "dp"), scatter_dimension=0, tiled=True),
    )
    (
        grad_b_query,
        grad_b_value,
        grad_b_out,
        grad_gain_one,
        grad_bias_one,
        grad_b_image,
        grad_cb_query,
        grad_cb_value,
        grad_cb_out,
        grad_gain_two,
        grad_bias_two,
        grad_b_inner,
        grad_b_outer,
        grad_gain_three,
        grad_bias_three,
    ) = lax.psum(
        (
            grad_b_query,
            grad_b_value,
            grad_b_out,
            grad_gain_one,
            grad_bias_one,
            grad_b_image,
            grad_cb_query,
            grad_cb_value,
            grad_cb_out,
            grad_gain_two,
            grad_bias_two,
            grad_b_inner,
            grad_b_outer,
            grad_gain_three,
            grad_bias_three,
        ),
        ("mod", "dp"),
    )
    return (
        mixed_out,
        grad_text.reshape(ITEMS_DEV, SEQ, D),
        grad_patches.reshape(ITEMS_DEV, NP, VW),
        grad_w_query,
        grad_w_key,
        grad_w_value,
        grad_w_out,
        grad_b_query,
        grad_b_value,
        grad_b_out,
        grad_gain_one,
        grad_bias_one,
        grad_w_image,
        grad_b_image,
        grad_c_query,
        grad_c_key,
        grad_c_value,
        grad_c_out,
        grad_cb_query,
        grad_cb_value,
        grad_cb_out,
        grad_gain_two,
        grad_bias_two,
        grad_w_inner,
        grad_b_inner,
        grad_w_outer,
        grad_b_outer,
        grad_gain_three,
        grad_bias_three,
    )


def solution(mesh):
    in_specs = (
        P(("mod", "dp"), None, None),
        P(("mod", "dp")),
        P(("mod", "dp"), None, None),
        P(("mod", "dp"), None),
        P(("mod", "dp"), None),
        P(("mod", "dp"), None),
        P(("mod", "dp"), None),
        P(),
        P(),
        P(),
        P(),
        P(),
        P(("mod", "dp"), None),
        P(),
        P(("mod", "dp"), None),
        P(("mod", "dp"), None),
        P(("mod", "dp"), None),
        P(("mod", "dp"), None),
        P(),
        P(),
        P(),
        P(),
        P(),
        P(("mod", "dp"), None),
        P(),
        P(("mod", "dp"), None),
        P(),
        P(),
        P(),
        P(("mod", "dp"), None, None),
    )
    out_specs = (
        P(("mod", "dp"), None, None),
        P(("mod", "dp"), None, None),
        P(("mod", "dp"), None, None),
        P(("mod", "dp"), None),
        P(("mod", "dp"), None),
        P(("mod", "dp"), None),
        P(("mod", "dp"), None),
        P(),
        P(),
        P(),
        P(),
        P(),
        P(("mod", "dp"), None),
        P(),
        P(("mod", "dp"), None),
        P(("mod", "dp"), None),
        P(("mod", "dp"), None),
        P(("mod", "dp"), None),
        P(),
        P(),
        P(),
        P(),
        P(),
        P(("mod", "dp"), None),
        P(),
        P(("mod", "dp"), None),
        P(),
        P(),
        P(),
    )
    return jax.shard_map(local, mesh=mesh, in_specs=in_specs, out_specs=out_specs, check_vma=False)
```

profile of v0, /device:TPU:0, one launch (start us, length us, event | category | flops | bytes accessed | tf_op | source)
XLA Modules:
  0.0 1901.2 jit_solution(4393808702830237186)
XLA Ops:
  19.6 48.2 %all-gather.14.cloned.1.call-done = bf16[768,768]{1,0:T(8,128)(2,1)} async-done(((bf16[24,768]{1,0:T(8,128)(2,1)}), bf16[768,768]{1,0:T(8,128)(2,1)}) %all-gather.14.cloned.1.call-update) | async-done | bytes 1179664 | tf_op jit(solution)/shard_map/all_gather | solution.py:153
  69.9 53.9 %all-gather.16.cloned.1.call-done = bf16[768,768]{1,0:T(8,128)(2,1)} async-done(((bf16[24,768]{1,0:T(8,128)(2,1)}), bf16[768,768]{1,0:T(8,128)(2,1)}) %all-gather.16.cloned.1.call-update) | async-done | bytes 1179664 | tf_op jit(solution)/shard_map/all_gather | solution.py:154
  126.6 53.0 %all-gather.12.cloned.1.call-done = bf16[768,768]{1,0:T(8,128)(2,1)} async-done(((bf16[24,768]{1,0:T(8,128)(2,1)}), bf16[768,768]{1,0:T(8,128)(2,1)}) %all-gather.12.cloned.1.call-update) | async-done | bytes 1179664 | tf_op jit(solution)/shard_map/all_gather | solution.py:155
  186.7 49.6 %all-gather.20.cloned.1.call-done = bf16[1024,768]{1,0:T(8,128)(2,1)} async-done(((bf16[32,768]{1,0:T(8,128)(2,1)}), bf16[1024,768]{1,0:T(8,128)(2,1)}) %all-gather.20.cloned.1.call-update) | async-done | bytes 1572880 | tf_op jit(solution)/shard_map/all_gather | solution.py:157
  239.2 52.9 %all-gather.22.cloned.1.call-done = bf16[768,768]{1,0:T(8,128)(2,1)} async-done(((bf16[24,768]{1,0:T(8,128)(2,1)}), bf16[768,768]{1,0:T(8,128)(2,1)}) %all-gather.22.cloned.1.call-update) | async-done | bytes 1179664 | tf_op jit(solution)/shard_map/all_gather | solution.py:160
  296.6 51.4 %all-gather.26.cloned.1.call-done = bf16[768,768]{1,0:T(8,128)(2,1)} async-done(((bf16[24,768]{1,0:T(8,128)(2,1)}), bf16[768,768]{1,0:T(8,128)(2,1)}) %all-gather.26.cloned.1.call-update) | async-done | bytes 1179664 | tf_op jit(solution)/shard_map/all_gather | solution.py:159
  352.5 51.6 %all-gather.18.cloned.1.call-done = bf16[768,768]{1,0:T(8,128)(2,1)} async-done(((bf16[24,768]{1,0:T(8,128)(2,1)}), bf16[768,768]{1,0:T(8,128)(2,1)}) %all-gather.18.cloned.1.call-update) | async-done | bytes 1179664 | tf_op jit(solution)/shard_map/all_gather | solution.py:156
  406.1 53.9 %all-gather.24.cloned.1.call-done = bf16[768,768]{1,0:T(8,128)(2,1)} async-done(((bf16[24,768]{1,0:T(8,128)(2,1)}), bf16[768,768]{1,0:T(8,128)(2,1)}) %all-gather.24.cloned.1.call-update) | async-done | bytes 1179664 | tf_op jit(solution)/shard_map/all_gather | solution.py:158
  489.3 26.6 %all-gather.28.cloned.1.call-done = bf16[768,768]{1,0:T(8,128)(2,1)} async-done(((bf16[24,768]{1,0:T(8,128)(2,1)}), bf16[768,768]{1,0:T(8,128)(2,1)}) %all-gather.28.cloned.1.call-update) | async-done | bytes 1179664 | tf_op jit(solution)/shard_map/all_gather | solution.py:161
  519.6 61.5 %all-gather.30.cloned.1.call-done = bf16[768,3072]{1,0:T(8,128)(2,1)} async-done(((bf16[24,3072]{1,0:T(8,128)(2,1)}), bf16[768,3072]{1,0:T(8,128)(2,1)}) %all-gather.30.cloned.1.call-update) | async-done | bytes 4718608 | tf_op jit(solution)/shard_map/all_gather | solution.py:183
  591.1 55.3 %all-gather.32.cloned.1.call-done = bf16[3072,768]{1,0:T(8,128)(2,1)} async-done(((bf16[96,768]{1,0:T(8,128)(2,1)}), bf16[3072,768]{1,0:T(8,128)(2,1)}) %all-gather.32.cloned.1.call-update) | async-done | bytes 4718608 | tf_op jit(solution)/shard_map/all_gather | solution.py:184
  714.2 25.1 %collective-permute-done.2 = bf16[580,768]{1,0:T(8,128)(2,1)S(1)} collective-permute-done((bf16[580,768]{1,0:T(8,128)(2,1)}, bf16[580,768]{1,0:T(8,128)(2,1)S(1)}, u32[]{:S(2)}, u32[]{:S(2)}) %collective-permute-start.2) | collective-permute-done | bytes 890912 | tf_op jit(solution)/shard_map/ppermute | solution.py:28
  759.0 20.6 %collective-permute-done.3 = bf16[580,768]{1,0:T(8,128)(2,1)S(1)} collective-permute-done((bf16[580,768]{1,0:T(8,128)(2,1)}, bf16[580,768]{1,0:T(8,128)(2,1)S(1)}, u32[]{:S(2)}, u32[]{:S(2)}) %collective-permute-start.3) | collective-permute-done | bytes 890912 | tf_op jit(solution)/shard_map/ppermute | solution.py:28
  820.8 42.4 %all-reduce = (f32[768]{0:T(1024)}, f32[768]{0:T(1024)}, f32[768]{0:T(1024)}, f32[768]{0:T(1024)}, f32[768]{0:T(1024)}, /*index=5*/f32[768]{0:T(1024)}, f32[768]...) all-reduce(f32[768]{0:T(1024)S(1)} %reduce_sum.350, ...), channel_id=1, replica_groups=mesh['mod'=2,'dp'=16] {'mod','dp'}, use_global_device_ids=true, to_apply=%region_23.24 | all-reduce | flops 13824 | bytes 110592 | tf_op jit(solution)/shard_map/psum | solution.py:291
  863.2 15.2 reduce-scatter.38.cloned.1.call-done
  878.5 103.9 %reduce-scatter.36.cloned.1.call-done = f32[24,768]{1,0:T(8,128)} async-done(((f32[768,768]{1,0:T(8,128)}), f32[24,768]{1,0:T(8,128)}) %reduce-scatter.36.cloned.1.call-update) | async-done | bytes 73744
  982.4 104.6 %reduce-scatter.34.cloned.1.call-done = f32[24,768]{1,0:T(8,128)} async-done(((f32[768,768]{1,0:T(8,128)}), f32[24,768]{1,0:T(8,128)}) %reduce-scatter.34.cloned.1.call-update) | async-done | bytes 73744
  1087.0 103.9 %reduce-scatter.20.cloned.1.call-done = f32[24,768]{1,0:T(8,128)} async-done(((f32[768,768]{1,0:T(8,128)}), f32[24,768]{1,0:T(8,128)}) %reduce-scatter.20.cloned.1.call-update) | async-done | bytes 73744 | tf_op jit(solution)/shard_map/reduce_scatter | solution.py:268
  1190.9 104.6 %reduce-scatter.28.cloned.1.call-done = f32[24,768]{1,0:T(8,128)} async-done(((f32[768,768]{1,0:T(8,128)}), f32[24,768]{1,0:T(8,128)}) %reduce-scatter.28.cloned.1.call-update) | async-done | bytes 73744 | tf_op jit(solution)/shard_map/reduce_scatter | solution.py:273
  1295.5 103.9 %reduce-scatter.24.cloned.1.call-done = f32[24,768]{1,0:T(8,128)} async-done(((f32[768,768]{1,0:T(8,128)}), f32[24,768]{1,0:T(8,128)}) %reduce-scatter.24.cloned.1.call-update) | async-done | bytes 73744 | tf_op jit(solution)/shard_map/reduce_scatter | solution.py:271
  1399.4 104.8 %reduce-scatter.26.cloned.1.call-done = f32[24,768]{1,0:T(8,128)} async-done(((f32[768,768]{1,0:T(8,128)}), f32[24,768]{1,0:T(8,128)}) %reduce-scatter.26.cloned.1.call-update) | async-done | bytes 73744 | tf_op jit(solution)/shard_map/reduce_scatter | solution.py:272
  1504.1 106.5 %reduce-scatter.40.cloned.1.call-done = f32[32,768]{1,0:T(8,128)} async-done(((f32[1024,768]{1,0:T(8,128)}), f32[32,768]{1,0:T(8,128)}) %reduce-scatter.40.cloned.1.call-update) | async-done | bytes 98320
  1610.6 141.1 %reduce-scatter.30.cloned.1.call-done = f32[24,3072]{1,0:T(8,128)} async-done(((f32[768,3072]{1,0:T(8,128)}), f32[24,3072]{1,0:T(8,128)}) %reduce-scatter.30.cloned.1.call-update) | async-done | bytes 294928 | tf_op jit(solution)/shard_map/reduce_scatter | solution.py:211
  1751.8 142.2 %reduce-scatter.32.cloned.1.call-done = f32[96,768]{1,0:T(8,128)} async-done(((f32[3072,768]{1,0:T(8,128)}), f32[96,768]{1,0:T(8,128)}) %reduce-scatter.32.cloned.1.call-update) | async-done | bytes 294928 | tf_op jit(solution)/shard_map/reduce_scatter | solution.py:212
  (374 shorter events, 208.6 us)
Async XLA Ops:
  7.2 60.6 %all-gather.14.cloned.1.call-start = ((), (), s32[]{:S(2)}) async-start(), calls=%async_computation.12 | async-start | bytes 1216512 | tf_op jit(solution)/shard_map/all_gather | solution.py:153
  7.9 115.8 %all-gather.16.cloned.1.call-start = ((), (), s32[]{:S(2)}) async-start(), calls=%async_computation.13 | async-start | bytes 1216512 | tf_op jit(solution)/shard_map/all_gather | solution.py:154
  8.7 171.0 %all-gather.12.cloned.1.call-start = ((), (), s32[]{:S(2)}) async-start(), calls=%async_computation.11 | async-start | bytes 1216512 | tf_op jit(solution)/shard_map/all_gather | solution.py:155
  9.4 226.9 %all-gather.20.cloned.1.call-start = ((), (), s32[]{:S(2)}) async-start(), calls=%async_computation.15 | async-start | bytes 1622016 | tf_op jit(solution)/shard_map/all_gather | solution.py:157
  10.0 282.1 %all-gather.22.cloned.1.call-start = ((), (), s32[]{:S(2)}) async-start(), calls=%async_computation.16 | async-start | bytes 1216512 | tf_op jit(solution)/shard_map/all_gather | solution.py:160
  10.6 337.4 %all-gather.26.cloned.1.call-start = ((), (), s32[]{:S(2)}) async-start(), calls=%async_computation.18 | async-start | bytes 1216512 | tf_op jit(solution)/shard_map/all_gather | solution.py:159
  11.2 392.9 %all-gather.18.cloned.1.call-start = ((), (), s32[]{:S(2)}) async-start(), calls=%async_computation.14 | async-start | bytes 1216512 | tf_op jit(solution)/shard_map/all_gather | solution.py:156
  11.9 448.1 %all-gather.24.cloned.1.call-start = ((), (), s32[]{:S(2)}) async-start(), calls=%async_computation.17 | async-start | bytes 1216512 | tf_op jit(solution)/shard_map/all_gather | solution.py:158
  12.7 503.3 %all-gather.28.cloned.1.call-start = ((), (), s32[]{:S(2)}) async-start(), calls=%async_computation.19 | async-start | bytes 1216512 | tf_op jit(solution)/shard_map/all_gather | solution.py:161
  13.4 567.7 %all-gather.30.cloned.1.call-start = ((), (), s32[]{:S(2)}) async-start(), calls=%async_computation.20 | async-start | bytes 4866048 | tf_op jit(solution)/shard_map/all_gather | solution.py:183
  14.0 632.4 %all-gather.32.cloned.1.call-start = ((), (), s32[]{:S(2)}) async-start(), calls=%async_computation.21 | async-start | bytes 4866048 | tf_op jit(solution)/shard_map/all_gather | solution.py:184
  14.7 848.5 %reduce-scatter.22.cloned.1.call-start = ((), (), s32[]{:S(2)}) async-start(), calls=%async_computation.23 | async-start | bytes 2433024 | tf_op jit(solution)/shard_map/reduce_scatter | solution.py:270
  295.2 174.1 %collective-permute-start = (bf16[580,768]{1,0:T(8,128)(2,1)}, bf16[580,768]{1,0:T(8,128)(2,1)}, u32[]{:S(2)}, u32[]{:S(2)}) collective-permute-start(bf16[580,768]{1,0:T(8,128)(2,1)} %add_convert_fusion.2), channel_id=1, source_target_pairs={{0,16},{16,0},{1,17},{17,1},{2,18},{18,2},{3,19},{19,3},{4,20},{20... | collective-permute-start | bytes 2672648 | tf_op jit(solution)/shard_map/ppermute | solution.py:28
  351.1 111.8 %collective-permute-start.1 = (bf16[580,768]{1,0:T(8,128)(2,1)}, bf16[580,768]{1,0:T(8,128)(2,1)S(1)}, u32[]{:S(2)}, u32[]{:S(2)}) collective-permute-start(bf16[580,768]{1,0:T(8,128)(2,1)} %convolution_convert_fusion.1), channel_id=1, source_target_pairs={{0,16},{16,0},{1,17},{17,1},{2,18},{18,2},{3,19},{19,3},{4,20},{20... | collective-permute-start | bytes 2672648 | tf_op jit(solution)/shard_map/ppermute | solution.py:28
  671.1 207.3 %reduce-scatter.38.cloned.1.call-start = ((), (), s32[]{:S(2)}) async-start(), calls=%async_computation.31 | async-start | bytes 2433024
  683.6 298.8 %reduce-scatter.36.cloned.1.call-start = ((), (), s32[]{:S(2)}) async-start(), calls=%async_computation.30 | async-start | bytes 2433024
  692.9 394.0 %reduce-scatter.34.cloned.1.call-start = ((), (), s32[]{:S(2)}) async-start(), calls=%async_computation.29 | async-start | bytes 2433024
  699.9 491.0 %reduce-scatter.20.cloned.1.call-start = ((), (), s32[]{:S(2)}) async-start(), calls=%async_computation.22 | async-start | bytes 2433024 | tf_op jit(solution)/shard_map/reduce_scatter | solution.py:268
  702.9 592.6 %reduce-scatter.28.cloned.1.call-start = ((), (), s32[]{:S(2)}) async-start(), calls=%async_computation.26 | async-start | bytes 2433024 | tf_op jit(solution)/shard_map/reduce_scatter | solution.py:273
  704.8 694.5 %reduce-scatter.24.cloned.1.call-start = ((), (), s32[]{:S(2)}) async-start(), calls=%async_computation.24 | async-start | bytes 2433024 | tf_op jit(solution)/shard_map/reduce_scatter | solution.py:271
  743.9 760.2 %reduce-scatter.26.cloned.1.call-start = ((), (), s32[]{:S(2)}) async-start(), calls=%async_computation.25 | async-start | bytes 2433024 | tf_op jit(solution)/shard_map/reduce_scatter | solution.py:272
  783.7 827.0 %reduce-scatter.40.cloned.1.call-start = ((), (), s32[]{:S(2)}) async-start(), calls=%async_computation.32 | async-start | bytes 3244032
  794.5 957.3 %reduce-scatter.30.cloned.1.call-start = ((), (), s32[]{:S(2)}) async-start(), calls=%async_computation.27 | async-start | bytes 9732096 | tf_op jit(solution)/shard_map/reduce_scatter | solution.py:211
  800.9 1093.0 %reduce-scatter.32.cloned.1.call-start = ((), (), s32[]{:S(2)}) async-start(), calls=%async_computation.28 | async-start | bytes 9732096 | tf_op jit(solution)/shard_map/reduce_scatter | solution.py:212
  (106 other events, 1941.9 us)
Sparse Core Ops, SparseCore 0:
  10.9 56.7 all-gather.13
  70.7 52.9 all-gather.15
  126.6 52.9 all-gather.11
  182.4 53.8 all-gather.19
  239.1 52.9 all-gather.21
  294.9 53.0 all-gather.25
  350.9 53.1 all-gather.17
  407.0 52.9 all-gather.23
  462.9 52.9 all-gather.27
  518.7 62.3 all-gather.29
  584.0 62.3 all-gather.31
  671.2 102.0 reduce-scatter.21
  780.0 98.3 reduce-scatter.37
  884.2 98.1 reduce-scatter.35
  988.9 98.0 reduce-scatter.33
  1092.7 98.1 reduce-scatter.19
  1197.4 98.0 reduce-scatter.27
  1301.2 98.0 reduce-scatter.23
  1406.1 98.0 reduce-scatter.25
  1510.0 100.5 reduce-scatter.39
  1617.1 134.5 reduce-scatter.29
  1759.2 134.6 reduce-scatter.31
where the time goes:
time: 1910 us; the launch traced here: 1900 us
  waiting for transfers between devices  1640 us (86%)
  matrix products  108 us (6%)
  local copies, waits for them, and re-layouts  72.9 us (4%)
  blocking collectives  42.4 us (2%)
    unnamed x26, waiting for transfers between devices  337 us
    reduce_scatter x1, waiting for transfers between devices, local(): lax.psum_scatter(grad_w_outer, ('mod', 'dp'), scatter_dimension=0, tiled=...  142 us
    reduce_scatter x1, waiting for transfers between devices, local(): lax.psum_scatter(grad_w_inner, ('mod', 'dp'), scatter_dimension=0, tiled=...  141 us
    reduce_scatter x1, waiting for transfers between devices, local(): lax.psum_scatter(grad_c_value, ('mod', 'dp'), scatter_dimension=0, tiled=...  105 us
    reduce_scatter x1, waiting for transfers between devices, local(): lax.psum_scatter(grad_c_out, ('mod', 'dp'), scatter_dimension=0, tiled=True)  105 us
    reduce_scatter x1, waiting for transfers between devices, local(): lax.psum_scatter(grad_w_out, ('mod', 'dp'), scatter_dimension=0, tiled=True)  104 us
    reduce_scatter x1, waiting for transfers between devices, local(): lax.psum_scatter(grad_c_key, ('mod', 'dp'), scatter_dimension=0, tiled=True)  104 us
    all_gather x1, waiting for transfers between devices, local(): lax.all_gather(w_inner, ('mod', 'dp'), axis=0, tiled=True)  61.5 us
  transfers between devices with their start and end apart: 26, of which 23 were waited for; matrix products, arithmetic and copies ran while one was open for 8% of the time, Pallas kernels for 0%

commit v1 on v0

v1 whole, which is shorter than its diff:
```python
import jax
import jax.numpy as jnp
from jax import lax
from jax.experimental import pallas as pl
from jax.experimental.pallas import tpu as pltpu
from jax.sharding import PartitionSpec as P

D = 768
HD = 64
GROUP = 256
NGROUP = 3
PER = 4
VW = 1024
NP = 145
SEQ = 40
ITEMS = 4
TP = 48
IP = 160
TR = ITEMS * TP
IR = ITEMS * IP
FF = 3072
HALF = D // 2
CHIPS = 16
LANES = CHIPS * 2
SCALE = HD**-0.5
neg_large = -1000000000.0
ln_eps = 1e-06
bf16 = jnp.bfloat16
f32 = jnp.float32
AXES = ("mod", "dp")

Y, Z0, Z1, X = 1, 2, 4, 8
ZS = (0, Z0, Z1, Z0 | Z1)


def layout_of(first):
    last = Y if first == X else X
    return [z for z in ZS] + [z ^ first for z in ZS], last


PIECES = {
    "qkv": ((48, 48, 48), X),
    "img": ((64, 48, 48), Y),
    "mid": ((48, 48, 48), X),
    "inner": ((48, 48, 48, 48), Y),
    "outer": ((192,), X),
}


def mm(a, b):
    return jnp.dot(a, b, preferred_element_type=f32)


def mm_t(a, b):
    return lax.dot_general(a, b, (((1,), (1,)), ((), ())), preferred_element_type=f32)


def mm_w(a, b):
    return lax.dot_general(a, b, (((0,), (0,)), ((), ())), preferred_element_type=f32)


def rowsum(a):
    return jnp.sum(a.astype(f32), axis=0, keepdims=True)


def ln_parts(v):
    centered = v - jnp.mean(v, axis=-1, keepdims=True)
    spread = jnp.mean(centered * centered, axis=-1, keepdims=True)
    scale = lax.rsqrt(spread + ln_eps)
    return centered * scale, scale


def ln_back(grad, normed, scale, gain):
    a = grad * gain
    inner = a - jnp.mean(a, axis=-1, keepdims=True)
    return scale * (inner - normed * jnp.mean(a * normed, axis=-1, keepdims=True))


def head_masks():
    head = lax.broadcasted_iota(jnp.int32, (1, GROUP), 1) // HD
    return [jnp.where(head == h, 1.0, 0.0) for h in range(PER)]


def expand(rows, masks):
    return jnp.concatenate([rows * m.astype(bf16) for m in masks], axis=0)


def collapse(full, masks):
    total = full[0:TP] * masks[0]
    for h in range(1, PER):
        total = total + full[h * TP : (h + 1) * TP] * masks[h]
    return total


def softmax_rows(scores):
    e = jnp.exp(scores - jnp.max(scores, axis=-1, keepdims=True))
    return e / jnp.sum(e, axis=-1, keepdims=True)


def attend_forward(q_ref, k_ref, v_ref, o_ref, key_rows, length_of):
    masks = head_masks()
    column = lax.broadcasted_iota(jnp.int32, (1, key_rows), 1)

    def item(i, carry):
        rows = pl.ds(pl.multiple_of(i * TP, 16), TP)
        keys = pl.ds(pl.multiple_of(i * key_rows, 16), key_rows)
        bias = jnp.where(column < length_of(i), 0.0, neg_large)
        for g in range(NGROUP):
            lanes = slice(g * GROUP, (g + 1) * GROUP)
            q = expand(q_ref[rows, lanes], masks)
            probs = softmax_rows(mm_t(q, k_ref[keys, lanes]) * SCALE + bias)
            out = mm(probs.astype(bf16), v_ref[keys, lanes])
            o_ref[rows, lanes] = collapse(out, masks).astype(bf16)
        return carry

    lax.fori_loop(0, ITEMS, item, 0)


def attend_backward(go_ref, q_ref, k_ref, v_ref, dq_ref, dk_ref, dv_ref, key_rows, length_of):
    masks = head_masks()
    column = lax.broadcasted_iota(jnp.int32, (1, key_rows), 1)

    def item(i, carry):
        rows = pl.ds(pl.multiple_of(i * TP, 16), TP)
        keys = pl.ds(pl.multiple_of(i * key_rows, 16), key_rows)
        bias = jnp.where(column < length_of(i), 0.0, neg_large)
        for g in range(NGROUP):
            lanes = slice(g * GROUP, (g + 1) * GROUP)
            q = expand(q_ref[rows, lanes], masks)
            k = k_ref[keys, lanes]
            probs = softmax_rows(mm_t(q, k) * SCALE + bias)
            go = expand(go_ref[rows, lanes], masks)
            dp = mm_t(go, v_ref[keys, lanes])
            ds = (probs * (dp - jnp.sum(probs * dp, axis=-1, keepdims=True))).astype(bf16)
            dq_ref[rows, lanes] = (collapse(mm(ds, k), masks) * SCALE).astype(bf16)
            dk_ref[keys, lanes] = (mm_w(ds, q) * SCALE).astype(bf16)
            dv_ref[keys, lanes] = mm_w(probs.astype(bf16), go).astype(bf16)
        return carry

    lax.fori_loop(0, ITEMS, item, 0)


def piece_kernel(body, piece, grads, meta, ins, outs):
    name, bufs = piece
    sizes, first = PIECES[name]
    rows = sum(sizes)
    base, last = layout_of(first)
    half = len(base)
    n_in, n_out = len(ins), len(outs)

    def kernel(*refs):
        meta_ref, refs = refs[0], refs[1:]
        in_refs, refs = refs[:n_in], refs[n_in:]
        buf_refs, refs = refs[:4], refs[4:]
        out_refs, refs = refs[:n_out], refs[n_out:]
        if grads:
            grad_refs, refs = refs[:4], refs[4:]
            w_ref, load_sem, g_ref, store_sem = refs
        else:
            w_ref, load_sem = refs
        chip, core = meta_ref[0], meta_ref[1]
        columns = [
            pl.ds(pl.multiple_of(core * HALF, 128), HALF),
            pl.ds(pl.multiple_of((1 - core) * HALF, 128), HALF),
        ]

        def copies(hbm, vmem, sem, out):
            made = []
            for side in range(2):
                for part in range(2):
                    for j in range(half):
                        at = chip ^ (base[j] ^ (last if part else 0))
                        outside = hbm[side * 2 + part].at[j]
                        inside = vmem.at[at, :, columns[side]]
                        pair = (inside, outside) if out else (outside, inside)
                        made.append(pltpu.make_async_copy(*pair, sem.at[len(made)]))
            return made

        loads = copies(buf_refs, w_ref, load_sem, False)
        for copy in loads:
            copy.start()

        def ready():
            for copy in loads:
                copy.wait()

        def weight(k):
            low = sum(sizes[:k])
            return w_ref[:, low : low + sizes[k], :].reshape(CHIPS * sizes[k], D)

        def put(k, value):
            low = sum(sizes[:k])
            g_ref[:, low : low + sizes[k], :] = value.astype(bf16).reshape(CHIPS, sizes[k], D)

        body(meta_ref, ready, weight, put, in_refs, out_refs)
        if grads:
            stores = copies(grad_refs, g_ref, store_sem, True)
            for copy in stores:
                copy.start()
            for copy in stores:
                copy.wait()

    vmem = pl.BlockSpec(memory_space=pltpu.VMEM)
    hbm = pl.BlockSpec(memory_space=pl.ANY)
    out_shape = list(outs)
    out_specs = [vmem] * n_out
    scratch = [pltpu.VMEM((CHIPS, rows, D), bf16), pltpu.SemaphoreType.DMA((4 * half,))]
    if grads:
        out_shape += [jax.ShapeDtypeStruct((half, rows, HALF), bf16)] * 4
        out_specs += [hbm] * 4
        scratch += [pltpu.VMEM((CHIPS, rows, D), bf16), pltpu.SemaphoreType.DMA((4 * half,))]
    return pl.pallas_call(
        kernel,
        out_shape=out_shape,
        in_specs=[pl.BlockSpec(memory_space=pltpu.SMEM)] + [vmem] * n_in + [hbm] * 4,
        out_specs=out_specs,
        scratch_shapes=scratch,
        compiler_params=pltpu.CompilerParams(vmem_limit_bytes=48 * 1024 * 1024),
        name=name + ("_back" if grads else "_front"),
    )(meta, *ins, *bufs)


def shape(*dims, dtype=bf16):
    return jax.ShapeDtypeStruct(dims, dtype)


def self_front(meta, ready, weight, put, ins, outs):
    text, b_query, b_value = ins
    q, k, v, attn = outs
    ready()
    rows = text[...]
    q[...] = (mm(rows, weight(0)) + b_query[...]).astype(bf16)
    k[...] = mm(rows, weight(1)).astype(bf16)
    v[...] = (mm(rows, weight(2)) + b_value[...]).astype(bf16)
    attend_forward(q, k, v, attn, TP, lambda i: meta[2 + i])


def image_front(meta, ready, weight, put, ins, outs):
    images, b_image, cb_value = ins
    image_rows, ck, cv = outs
    ready()
    image_rows[...] = (mm(images[...], weight(0)) + b_image[...]).astype(bf16)
    ck[...] = mm(image_rows[...], weight(1)).astype(bf16)
    cv[...] = (mm(image_rows[...], weight(2)) + cb_value[...]).astype(bf16)


def mid_front(meta, ready, weight, put, ins, outs):
    text, attn, ck, cv, b_out, gain_one, bias_one, cb_query, cb_out, gain_two, bias_two = ins
    hidden, cq, cross, joint, sum_one, sum_two = outs
    ready()
    sum_one[...] = text[...].astype(f32) + (mm(attn[...], weight(0)) + b_out[...])
    normed, _ = ln_parts(sum_one[...])
    hidden[...] = (normed * gain_one[...] + bias_one[...]).astype(bf16)
    cq[...] = (mm(hidden[...], weight(1)) + cb_query[...]).astype(bf16)
    attend_forward(cq, ck, cv, cross, IP, lambda i: NP)
    sum_two[...] = hidden[...].astype(f32) + (mm(cross[...], weight(2)) + cb_out[...])
    normed, _ = ln_parts(sum_two[...])
    joint[...] = (normed * gain_two[...] + bias_two[...]).astype(bf16)


def inner_front(meta, ready, weight, put, ins, outs):
    joint, b_inner = ins
    active, slope = outs
    ready()
    for k in range(4):
        lanes = slice(k * D, (k + 1) * D)
        pre = mm(joint[...], weight(k)) + b_inner[:, lanes]
        cdf = 0.5 * (1.0 + lax.erf(pre * 0.5**0.5))
        active[:, lanes] = (pre * cdf).astype(bf16)
        slope[:, lanes] = cdf + pre * (jnp.exp(-0.5 * pre * pre) * 0.3989422804014327)


def outer_both(meta, ready, weight, put, ins, outs):
    active, slope, joint, cot, b_outer, gain, bias = ins
    mixed, grad_sum, grad_inner, vec = outs
    ready()
    normed, scale = ln_parts(joint[...].astype(f32) + (mm(active[...], weight(0)) + b_outer[...]))
    result = normed * gain[...] + bias[...]
    row = lax.broadcasted_iota(jnp.int32, (TP, 1), 0)
    keep = [jnp.where(row < meta[2 + i], 1.0, 0.0) for i in range(ITEMS)]
    for i in range(ITEMS):
        mixed[i] = (result[i * TP : (i + 1) * TP] * keep[i])[:SEQ]
    grad = cot[...].astype(f32) * jnp.concatenate(keep, axis=0)
    grad_sum[...] = ln_back(grad, normed, scale, gain[...])
    grad_outer = grad_sum[...].astype(bf16)
    vec[0:1] = rowsum(grad * normed)
    vec[1:2] = rowsum(grad)
    vec[2:3] = rowsum(grad_outer)
    vec[3:4] = jnp.zeros((1, D), f32)
    put(0, mm_w(active[...], grad_outer))
    for k in range(4):
        lanes = slice(k * D, (k + 1) * D)
        back = mm_t(grad_outer, weight(0)[k * D : (k + 1) * D])
        part = (slope[:, lanes] * back).astype(bf16)
        grad_inner[:, lanes] = part
        vec[4 + k : 5 + k] = rowsum(part)


def inner_back(meta, ready, weight, put, ins, outs):
    joint, grad_inner, grad_sum_three, sum_two, gain = ins
    grad_sum_two, vec = outs
    for k in range(4):
        put(k, mm_w(joint[...], grad_inner[:, k * D : (k + 1) * D]))
    ready()
    grad = grad_sum_three[...]
    for k in range(4):
        grad = grad + mm_t(grad_inner[:, k * D : (k + 1) * D], weight(k))
    normed, scale = ln_parts(sum_two[...])
    grad_sum_two[...] = ln_back(grad, normed, scale, gain[...])
    vec[...] = jnp.concatenate([rowsum(grad * normed), rowsum(grad), jnp.zeros((6, D), f32)], axis=0)


def mid_back(meta, ready, weight, put, ins, outs):
    grad_sum_two, cross, hidden, attn, cq, ck, cv, sum_one, gain = ins
    grad_sum_one, grad_attn, dk, dv, dq, vec = outs
    grad_cross_branch = grad_sum_two[...].astype(bf16)
    put(2, mm_w(cross[...], grad_cross_branch))
    ready()
    grad_attn[...] = mm_t(grad_cross_branch, weight(2)).astype(bf16)
    attend_backward(grad_attn, cq, ck, cv, dq, dk, dv, IP, lambda i: NP)
    put(1, mm_w(hidden[...], dq[...]))
    grad = grad_sum_two[...] + mm_t(dq[...], weight(1))
    normed, scale = ln_parts(sum_one[...])
    grad_sum_one[...] = ln_back(grad, normed, scale, gain[...])
    grad_branch = grad_sum_one[...].astype(bf16)
    put(0, mm_w(attn[...], grad_branch))
    grad_attn[...] = mm_t(grad_branch, weight(0)).astype(bf16)
    vec[...] = jnp.concatenate(
        [
            rowsum(grad_cross_branch),
            rowsum(dq[...]),
            rowsum(grad * normed),
            rowsum(grad),
            rowsum(grad_branch),
            jnp.zeros((3, D), f32),
        ],
        axis=0,
    )


def image_back(meta, ready, weight, put, ins, outs):
    images, image_rows, dk, dv = ins
    grad_patches, vec = outs
    put(1, mm_w(image_rows[...], dk[...]))
    put(2, mm_w(image_rows[...], dv[...]))
    ready()
    grad_image = (mm_t(dk[...], weight(1)) + mm_t(dv[...], weight(2))).astype(bf16)
    put(0, mm_w(images[...], grad_image))
    for i in range(ITEMS):
        grad_patches[i] = mm_t(grad_image[i * IP : (i + 1) * IP], weight(0))[:NP]
    vec[...] = jnp.concatenate([rowsum(dv[...]), rowsum(grad_image), jnp.zeros((6, D), f32)], axis=0)


def self_back(meta, ready, weight, put, ins, outs):
    grad_attn, q, k, v, text, grad_sum_one = ins
    grad_text, dq, dk, dv, vec = outs
    attend_backward(grad_attn, q, k, v, dq, dk, dv, TP, lambda i: meta[2 + i])
    put(0, mm_w(text[...], dq[...]))
    put(1, mm_w(text[...], dk[...]))
    put(2, mm_w(text[...], dv[...]))
    ready()
    total = grad_sum_one[...] + mm_t(dq[...], weight(0))
    total = total + mm_t(dk[...], weight(1))
    grad_text[...] = (total + mm_t(dv[...], weight(2))).astype(bf16)
    vec[...] = jnp.concatenate([rowsum(dq[...]), rowsum(dv[...]), jnp.zeros((6, D), f32)], axis=0)


def local(
    text,
    lengths,
    patches,
    w_query,
    w_key,
    w_value,
    w_out,
    b_query,
    b_value,
    b_out,
    gain_one,
    bias_one,
    w_image,
    b_image,
    c_query,
    c_key,
    c_value,
    c_out,
    cb_query,
    cb_value,
    cb_out,
    gain_two,
    bias_two,
    w_inner,
    b_inner,
    w_outer,
    b_outer,
    gain_three,
    bias_three,
    cotangent,
):
    count = lax.axis_size("mod") * lax.axis_size("dp")
    fold = count // LANES
    device = lax.axis_index("mod") * lax.axis_size("dp") + lax.axis_index("dp")
    place = device // fold
    core, chip = place % 2, place // 2
    first_core = core == 0

    def flip_device(block, mask):
        return lax.ppermute(block, AXES, [(i, i ^ mask) for i in range(count)])

    def flip_chip(block, mask):
        return flip_device(block, mask * 2 * fold)

    def flip_core(block):
        return flip_device(block, fold)

    def swap(block):
        return lax.ppermute(block, "mod", [(0, 1), (1, 0)])

    def gather_fold(shard):
        step = 1
        while step < fold:
            other = flip_device(shard, step)
            low = (device // step) % 2 == 0
            shard = jnp.concatenate(
                [jnp.where(low, shard, other), jnp.where(low, other, shard)], axis=0
            )
            step *= 2
        return shard

    def scatter_fold(total):
        step = fold // 2
        while step >= 1:
            low = (device // step) % 2 == 0
            half = total.shape[0] // 2
            kept = jnp.where(low, total[:half], total[half:])
            total = kept + flip_device(jnp.where(low, total[half:], total[:half]), step)
            step //= 2
        return total

    def gather_piece(name, shards):
        sizes, first = PIECES[name]
        shards = [gather_fold(s) for s in shards]
        lows, highs = [s[:, :HALF] for s in shards], [s[:, HALF:] for s in shards]
        kept = [jnp.where(first_core, a, b) for a, b in zip(lows, highs)]
        sent = jnp.concatenate([jnp.where(first_core, b, a) for a, b in zip(lows, highs)], axis=0)
        came = flip_core(sent)
        parts, at = [], 0
        for mine, size in zip(kept, sizes):
            theirs = came[at : at + size // 2]
            at += size // 2
            parts += [jnp.where(first_core, mine, theirs), jnp.where(first_core, theirs, mine)]
        block = jnp.concatenate(parts, axis=0)
        blocks = jnp.stack([block] + [flip_chip(block, z) for z in ZS[1:]])
        _, last = layout_of(first)
        own_0 = jnp.concatenate([blocks, flip_chip(blocks, first)], axis=0)
        own_1 = flip_chip(own_0, last)
        return name, (own_0, own_1, flip_core(own_0), flip_core(own_1))

    def reduce_piece(name, bufs):
        sizes, first = PIECES[name]
        _, last = layout_of(first)
        keep_0, keep_1, send_0, send_1 = bufs
        came_1 = flip_core(send_1)
        came_0 = flip_core(send_0)
        far = flip_chip((keep_1.astype(f32) + came_1.astype(f32)).astype(bf16), last)
        near = keep_0.astype(f32) + came_0.astype(f32) + far.astype(f32)
        across = flip_chip(near[4:].astype(bf16), first)
        blocks = (near[:4] + across.astype(f32)).astype(bf16)
        total = blocks[0].astype(f32)
        for j in range(1, 4):
            total = total + flip_chip(blocks[j], ZS[j]).astype(f32)
        at, mine, theirs = 0, [], []
        for size in sizes:
            a, b = total[at : at + size // 2], total[at + size // 2 : at + size]
            mine.append(jnp.where(first_core, a, b))
            theirs.append(jnp.where(first_core, b, a))
            at += size
        came = flip_core(jnp.concatenate(theirs, axis=0))
        result, at = [], 0
        for part in mine:
            other = came[at : at + part.shape[0]]
            at += part.shape[0]
            joined = [jnp.where(first_core, part, other), jnp.where(first_core, other, part)]
            result.append(scatter_fold(jnp.concatenate(joined, axis=1)))
        return result

    def sum_all(total):
        step = 1
        while step < 2 * fold * Y * 2:
            total = total + flip_device(total, step)
            step *= 2
        total = total + flip_chip(total, X)
        return total + flip_chip(total, Z0) + (flip_chip(total, Z1) + flip_chip(total, Z0 | Z1))

    def row(vector):
        return vector.reshape(1, -1)

    text_rows = swap(jnp.pad(text, ((0, 0), (0, TP - SEQ), (0, 0))).reshape(TR, D))
    item_lengths = swap(lengths)
    meta = jnp.concatenate([chip[None], core[None], item_lengths]).astype(jnp.int32)
    qkv = gather_piece("qkv", [w_query, w_key, w_value])
    img = gather_piece("img", [w_image, c_key, c_value])
    mid = gather_piece("mid", [w_out, c_query, c_out])
    inner = gather_piece("inner", [w_inner[:, k * D : (k + 1) * D] for k in range(4)])
    outer = gather_piece("outer", [w_outer])
    cot_rows = swap(jnp.pad(cotangent, ((0, 0), (0, TP - SEQ), (0, 0))).reshape(TR, D))
    images = jnp.pad(patches, ((0, 0), (0, IP - NP), (0, 0))).reshape(IR, VW)

    text_shape, image_shape = shape(TR, D), shape(IR, D)
    wide = shape(TR, D, dtype=f32)
    vec_shape = shape(8, D, dtype=f32)
    q, k, v, attn = piece_kernel(
        self_front, qkv, False, meta, [text_rows, row(b_query), row(b_value)], [text_shape] * 4
    )
    image_rows, ck, cv = piece_kernel(
        image_front, img, False, meta, [images, row(b_image), row(cb_value)], [image_shape] * 3
    )
    mid_params = [b_out, gain_one, bias_one, cb_query, cb_out, gain_two, bias_two]
    hidden, cq, cross, joint, sum_one, sum_two = piece_kernel(
        mid_front,
        mid,
        False,
        meta,
        [text_rows, attn, ck, cv] + [row(p) for p in mid_params],
        [text_shape] * 4 + [wide] * 2,
    )
    active, slope = piece_kernel(
        inner_front,
        inner,
        False,
        meta,
        [joint, row(b_inner)],
        [shape(TR, FF), shape(TR, FF, dtype=f32)],
    )
    mixed, grad_sum_three, grad_inner, vec_outer, *outer_grads = piece_kernel(
        outer_both,
        outer,
        True,
        meta,
        [active, slope, joint, cot_rows, row(b_outer), row(gain_three), row(bias_three)],
        [shape(ITEMS, SEQ, D, dtype=f32), wide, shape(TR, FF), vec_shape],
    )
    mixed_out = swap(mixed)
    (grad_w_outer,) = reduce_piece("outer", outer_grads)
    grad_sum_two, vec_inner, *inner_grads = piece_kernel(
        inner_back,
        inner,
        True,
        meta,
        [joint, grad_inner, grad_sum_three, sum_two, row(gain_two)],
        [wide, vec_shape],
    )
    grad_w_inner = jnp.concatenate(reduce_piece("inner", inner_grads), axis=1)
    grad_sum_one, grad_attn, dk, dv, _, vec_mid, *mid_grads = piece_kernel(
        mid_back,
        mid,
        True,
        meta,
        [grad_sum_two, cross, hidden, attn, cq, ck, cv, sum_one, row(gain_one)],
        [wide, text_shape, image_shape, image_shape, text_shape, vec_shape],
    )
    grad_w_out, grad_c_query, grad_c_out = reduce_piece("mid", mid_grads)
    grad_patches, vec_image, *img_grads = piece_kernel(
        image_back,
        img,
        True,
        meta,
        [images, image_rows, dk, dv],
        [shape(ITEMS, NP, VW, dtype=f32), vec_shape],
    )
    grad_w_image, grad_c_key, grad_c_value = reduce_piece("img", img_grads)
    grad_text, _, _, _, vec_self, *qkv_grads = piece_kernel(
        self_back,
        qkv,
        True,
        meta,
        [grad_attn, q, k, v, text_rows, grad_sum_one],
        [text_shape] * 4 + [vec_shape],
    )
    grad_w_query, grad_w_key, grad_w_value = reduce_piece("qkv", qkv_grads)
    grad_text = swap(grad_text).reshape(ITEMS, TP, D)[:, :SEQ].astype(f32)
    vecs = sum_all(jnp.concatenate([vec_outer, vec_inner, vec_mid, vec_image, vec_self], axis=0))
    grad_b_inner = vecs[4:8].reshape(FF)
    return (
        mixed_out,
        grad_text,
        grad_patches,
        grad_w_query,
        grad_w_key,
        grad_w_value,
        grad_w_out,
        vecs[32],
        vecs[33],
        vecs[20],
        vecs[18],
        vecs[19],
        grad_w_image,
        vecs[25],
        grad_c_query,
        grad_c_key,
        grad_c_value,
        grad_c_out,
        vecs[17],
        vecs[24],
        vecs[16],
        vecs[8],
        vecs[9],
        grad_w_inner,
        grad_b_inner,
        grad_w_outer,
        vecs[2],
        vecs[0],
        vecs[1],
    )


def solution(mesh):
    items = P(AXES, None, None)
    shard, whole = P(AXES, None), P()
    in_specs = (
        (items, P(AXES), items)
        + (shard,) * 4
        + (whole,) * 5
        + (shard, whole)
        + (shard,) * 4
        + (whole,) * 5
        + (shard, whole, shard)
        + (whole,) * 3
        + (items,)
    )
    out_specs = (
        (items,) * 3
        + (shard,) * 4
        + (whole,) * 5
        + (shard, whole)
        + (shard,) * 4
        + (whole,) * 5
        + (shard, whole, shard)
        + (whole,) * 3
    )
    return jax.shard_map(local, mesh=mesh, in_specs=in_specs, out_specs=out_specs, check_vma=False)
```

time: 1910 us -> 517 us (0.27)
  waiting for transfers between devices: 1640 us -> 247 us
  matrix products: 108 us -> 0 us
  Pallas kernels: 0 us -> 91.7 us
  starting transfers between devices: 7.14 us -> 83.4 us
  blocking collectives: 42.4 us -> 0 us
    reduce_scatter x7 -> x0, waiting for transfers between devices: 700 us -> none  [the longest x1 142 us: local(): lax.psum_scatter(grad_w_outer, ('mod', 'dp'), scatter_dimension=0, tiled=...]
    all_gather x11 -> x0, waiting for transfers between devices: 558 us -> none  [the longest x1 61.5 us: local(): lax.all_gather(w_inner, ('mod', 'dp'), axis=0, tiled=True)]
    unnamed x26 -> x0, waiting for transfers between devices: 337 us -> none
    ppermute x4 -> x91, waiting for transfers between devices: 45.7 us -> 247 us  [the longest x86 242 us: flip_device(): return lax.ppermute(block, AXES, [(i, i ^ mask) for i in range(count)])]
    dot_general x45 -> x0, matrix products: 108 us -> none  [the longest x11 32.9 us: project(): return jnp.dot(left_rows, weight, preferred_element_type=jnp.float32)]
    pallas_call x0 -> x9, Pallas kernels: none -> 91.7 us  [piece_kernel(): pl.pallas_call(kernel, out_shape=out_shape, in_specs=[pl.BlockSpec(memory...]
    ppermute x4 -> x91, starting transfers between devices: 5.63 us -> 83.4 us  [the longest x86 75.5 us: flip_device(): return lax.ppermute(block, AXES, [(i, i ^ mask) for i in range(count)])]
    psum x1 -> x0, blocking collectives: 42.4 us -> none  [local(): lax.psum((grad_b_query, grad_b_value, grad_b_out, grad_gain_one, grad_bia...]
  transfers between devices with their start and end apart: 26 -> 91, of which waited for: 23 -> 39; matrix products, arithmetic and copies ran while one was open for 8% -> 10% of each run, Pallas kernels for 0% -> 5%
where the time goes in v1:
time: 517 us; the launch traced here: 510 us
  waiting for transfers between devices  247 us (48%)
  Pallas kernels  91.7 us (18%)
  starting transfers between devices  83.4 us (16%)
  local copies, waits for them, and re-layouts  57.5 us (11%)
  other arithmetic  26.8 us (5%)
    ppermute x86, waiting for transfers between devices, flip_device(): return lax.ppermute(block, AXES, [(i, i ^ mask) for i in range(count)])  242 us
    pallas_call x9, Pallas kernels, piece_kernel(): pl.pallas_call(kernel, out_shape=out_shape, in_specs=[pl.BlockSpec(memory...  91.7 us
    ppermute x86, starting transfers between devices, flip_device(): return lax.ppermute(block, AXES, [(i, i ^ mask) for i in range(count)])  75.5 us
    unnamed x202, local copies, waits for them, and re-layouts  37.9 us
    reshape x14, local copies, waits for them, and re-layouts, row(): return vector.reshape(1, -1)  13.4 us
  transfers between devices with their start and end apart: 91, of which 39 were waited for; matrix products, arithmetic and copies ran while one was open for 10% of the time, Pallas kernels for 5%

profile of v1, /device:TPU:0, one launch (start us, length us, event | category | flops | bytes accessed | tf_op | source)
XLA Modules:
  0.0 509.7 jit_solution(12285005722611160359)
XLA Ops:
  56.7 7.5 %collective-permute-done.36 = bf16[192,384]{1,0:T(8,128)(2,1)S(1)} collective-permute-done((bf16[192,384]{1,0:T(8,128)(2,1)S(1)}, bf16[192,384]{1,0:T(8,128)(2,1)S(1)}, u32[]{:S(2)}, u32[]{:S(2)}) %collective-permute-start.36) | collective-permute-done | bytes 147488 | tf_op jit(solution)/shard_map/ppermute | solution.py:408
  64.9 6.8 %collective-permute-done.37 = bf16[192,384]{1,0:T(8,128)(2,1)S(1)} collective-permute-done((bf16[192,384]{1,0:T(8,128)(2,1)S(1)}, bf16[192,384]{1,0:T(8,128)(2,1)S(1)}, u32[]{:S(2)}, u32[]{:S(2)}) %collective-permute-start.37) | collective-permute-done | bytes 147488 | tf_op jit(solution)/shard_map/ppermute | solution.py:408
  84.3 7.5 %collective-permute-done.6 = bf16[4,144,384]{2,1,0:T(8,128)(2,1)S(1)} collective-permute-done((bf16[4,144,384]{2,1,0:T(8,128)(2,1)S(1)}, bf16[4,144,384]{2,1,0:T(8,128)(2,1)S(1)}, u32[]{:S(2)}, u32[]{:S(2)}) %collective-permute-start.6) | collective-permute-done | bytes 442400 | tf_op jit(solution)/shard_map/ppermute | solution.py:408
  92.4 5.7 %collective-permute-done.1.refs_1_.refs_5_ = bf16[192,768]{1,0:T(8,128)(2,1)S(1)} collective-permute-done((bf16[192,768]{1,0:T(8,128)(2,1)S(1)}, bf16[192,768]{1,0:T(8,128)(2,1)S(1)}, u32[]{:S(2)}, u32[]{:S(2)}) %collective-permute-start.1) | collective-permute-done | bytes 294944 | tf_op jit(solution)/shard_map/ppermute | solution.py:417
  112.6 13.6 %collective-permute-done.7.refs_5_.refs_8_ = bf16[8,144,384]{2,1,0:T(8,128)(2,1)S(1)} collective-permute-done((bf16[8,144,384]{2,1,0:T(8,128)(2,1)S(1)}, bf16[8,144,384]{2,1,0:T(8,128)(2,1)S(1)}, u32[]{:S(2)}, u32[]{:S(2)}) %collective-permute-start.7) | collective-permute-done | bytes 884768 | tf_op jit(solution)/shard_map/ppermute | solution.py:408
  129.2 16.0 %collective-permute-done.23.refs_13_.refs_11_ = bf16[8,144,384]{2,1,0:T(8,128)(2,1)S(1)} collective-permute-done((bf16[8,144,384]{2,1,0:T(8,128)(2,1)S(1)}, bf16[8,144,384]{2,1,0:T(8,128)(2,1)S(1)}, u32[]{:S(2)}, u32[]{:S(2)}) %collective-permute-start.23) | collective-permute-done | bytes 884768 | tf_op jit(solution)/shard_map/ppermute | solution.py:408
  148.6 12.9 %collective-permute-done.15.refs_5_.refs_6_ = bf16[8,160,384]{2,1,0:T(8,128)(2,1)S(1)} collective-permute-done((bf16[8,160,384]{2,1,0:T(8,128)(2,1)S(1)}, bf16[8,160,384]{2,1,0:T(8,128)(2,1)S(1)}, u32[]{:S(2)}, u32[]{:S(2)}) %collective-permute-start.15) | collective-permute-done | bytes 983072 | tf_op jit(solution)/shard_map/ppermute | solution.py:408
  192.4 6.3 %qkv_front.1 = (bf16[192,768]{1,0:T(8,128)(2,1)S(1)}, bf16[192,768]{1,0:T(8,128)(2,1)S(1)}, bf16[192,768]{1,0:T(8,128)(2,1)S(1)}, bf16[192,768]{1,0:T(8,128)(2,1)S(1)}) custom-call(s32[6]{0:T(128)S(1)} %pad_add_fusion.refs_0_, bf16[192,768]{1,0:T(8,128)(2,1)S(1)} %copy-done.26, f32[1,768]{1,0:T(1,128)S(1)} %copy-done.55, f32[1,768]{1,0:T(1,128)S(1)} %copy-done.56, ...), custom_call_target="tpu_custom_call" | custom-call | tf_op jit(solution)/shard_map/qkv_front/pallas_call | solution.py:212
  198.8 6.8 %img_front.1 = (bf16[640,768]{1,0:T(8,128)(2,1)S(1)}, bf16[640,768]{1,0:T(8,128)(2,1)S(1)}, bf16[640,768]{1,0:T(8,128)(2,1)S(1)}) custom-call(s32[6]{0:T(128)S(1)} %pad_add_fusion.refs_0_, bf16[640,1024]{1,0:T(8,128)(2,1)} %bitcast.104, f32[1,768]{1,0:T(1,128)S(1)} %copy-done.53, f32[1,768]{1,0:T(1,128)S(1)} %copy-done.54, ...), custom_call_target="tpu_custom_call" | custom-call | tf_op jit(solution)/shard_map/img_front/pallas_call | solution.py:212
  208.6 8.8 %mid_front.1 = (bf16[192,768]{1,0:T(8,128)(2,1)S(1)}, bf16[192,768]{1,0:T(8,128)(2,1)S(1)}, bf16[192,768]{1,0:T(8,128)(2,1)S(1)}, bf16[192,768]{1,0:T(8,128)(2,1...) custom-call(s32[6]{0:T(128)S(1)} %pad_add_fusion.refs_0_, bf16[192,768]{1,0:T(8,128)(2,1)S(1)} %copy-done.27, ...), custom_call_target="tpu_custom_call" | custom-call | tf_op jit(solution)/shard_map/mid_front/pallas_call | solution.py:212
  217.5 5.6 %inner_front.1 = (bf16[192,3072]{1,0:T(8,128)(2,1)S(1)}, f32[192,3072]{1,0:T(8,128)}) custom-call(s32[6]{0:T(128)S(1)} %pad_add_fusion.refs_0_, bf16[192,768]{1,0:T(8,128)(2,1)S(1)} %get-tuple-element.82.refs_1_.refs_3_, f32[1,3072]{1,0:T(1,128)S(1)} %bitcast.103, bf16[8,192,384]{2,1,0:T(8,128)(2,1)S(1)} %constant_dynamic-update-slice_fusion.41.refs_3_.refs_6_, ...), custom_call_target="tpu_custom_call" | custom-call | tf_op jit(solution)/shard_map/inner_front/pallas_call | solution.py:212
  224.2 11.8 %outer_back.1 = (f32[4,40,768]{2,1,0:T(8,128)S(1)}, f32[192,768]{1,0:T(8,128)S(1)}, bf16[192,3072]{1,0:T(8,128)(2,1)S(1)}, f32[8,768]{1,0:T(8,128)S(1)}, bf16[8,...) custom-call(s32[6]{0:T(128)S(1)} %pad_add_fusion.refs_0_, ...), custom_call_target="tpu_custom_call" | custom-call | tf_op jit(solution)/shard_map/outer_back/pallas_call | solution.py:212
  237.0 9.2 %inner_back.1 = (f32[192,768]{1,0:T(8,128)S(1)}, f32[8,768]{1,0:T(8,128)S(1)}, bf16[8,192,384]{2,1,0:T(8,128)(2,1)S(1)}, bf16[8,192,384]{2,1,0:T(8,128)(2,1)S(1)...) custom-call(s32[6]{0:T(128)S(1)} %pad_add_fusion.refs_0_, ...), custom_call_target="tpu_custom_call" | custom-call | tf_op jit(solution)/shard_map/inner_back/pallas_call | solution.py:212
  248.3 16.3 %mid_back.1 = (f32[192,768]{1,0:T(8,128)S(1)}, bf16[192,768]{1,0:T(8,128)(2,1)S(1)}, bf16[640,768]{1,0:T(8,128)(2,1)}, bf16[640,768]{1,0:T(8,128)(2,1)}, bf16[19...) custom-call(s32[6]{0:T(128)S(1)} %pad_add_fusion.refs_0_, ...), custom_call_target="tpu_custom_call" | custom-call | tf_op jit(solution)/shard_map/mid_back/pallas_call | solution.py:212
  268.7 13.5 %img_back.1 = (f32[4,145,1024]{2,1,0:T(8,128)}, f32[8,768]{1,0:T(8,128)S(1)}, bf16[8,160,384]{2,1,0:T(8,128)(2,1)S(1)}, bf16[8,160,384]{2,1,0:T(8,128)(2,1)S(1)}...) custom-call(s32[6]{0:T(128)S(1)} %pad_add_fusion.refs_0_, bf16[640,1024]{1,0:T(8,128)(2,1)} %bitcast.105, ...), custom_call_target="tpu_custom_call" | custom-call | tf_op jit(solution)/shard_map/img_back/pallas_call | solution.py:212
  285.1 13.3 %qkv_back.1 = (bf16[192,768]{1,0:T(8,128)(2,1)S(1)}, bf16[192,768]{1,0:T(8,128)(2,1)}, bf16[192,768]{1,0:T(8,128)(2,1)}, bf16[192,768]{1,0:T(8,128)(2,1)}, f32[8...) custom-call(s32[6]{0:T(128)S(1)} %pad_add_fusion.refs_0_, ...), custom_call_target="tpu_custom_call" | custom-call | tf_op jit(solution)/shard_map/qkv_back/pallas_call | solution.py:212
  306.9 14.2 %collective-permute-done.63 = f32[40,768]{1,0:T(8,128)S(1)} collective-permute-done((f32[40,768]{1,0:T(8,128)S(1)}, f32[40,768]{1,0:T(8,128)S(1)}, u32[]{:S(2)}, u32[]{:S(2)}) %collective-permute-start.63) | collective-permute-done | bytes 122912 | tf_op jit(solution)/shard_map/ppermute | solution.py:408
  349.8 15.3 %collective-permute-done.47 = bf16[8,144,384]{2,1,0:T(8,128)(2,1)S(1)} collective-permute-done((bf16[8,144,384]{2,1,0:T(8,128)(2,1)S(1)}, bf16[8,144,384]{2,1,0:T(8,128)(2,1)S(1)}, u32[]{:S(2)}, u32[]{:S(2)}) %collective-permute-start.47) | collective-permute-done | bytes 884768 | tf_op jit(solution)/shard_map/ppermute | solution.py:408
  368.2 15.4 %collective-permute-done.55 = bf16[8,144,384]{2,1,0:T(8,128)(2,1)S(1)} collective-permute-done((bf16[8,144,384]{2,1,0:T(8,128)(2,1)S(1)}, bf16[8,144,384]{2,1,0:T(8,128)(2,1)S(1)}, u32[]{:S(2)}, u32[]{:S(2)}) %collective-permute-start.55) | collective-permute-done | bytes 884768 | tf_op jit(solution)/shard_map/ppermute | solution.py:408
  386.7 20.6 %collective-permute-done.48 = bf16[4,144,384]{2,1,0:T(8,128)(2,1)S(1)} collective-permute-done((bf16[4,144,384]{2,1,0:T(8,128)(2,1)S(1)}, bf16[4,144,384]{2,1,0:T(8,128)(2,1)S(1)}, u32[]{:S(2)}, u32[]{:S(2)}) %collective-permute-start.48) | collective-permute-done | bytes 442400 | tf_op jit(solution)/shard_map/ppermute | solution.py:408
  410.2 6.2 %collective-permute-done.56 = bf16[4,144,384]{2,1,0:T(8,128)(2,1)S(1)} collective-permute-done((bf16[4,144,384]{2,1,0:T(8,128)(2,1)S(1)}, bf16[4,144,384]{2,1,0:T(8,128)(2,1)S(1)}, u32[]{:S(2)}, u32[]{:S(2)}) %collective-permute-start.56) | collective-permute-done | bytes 442400 | tf_op jit(solution)/shard_map/ppermute | solution.py:408
  436.7 5.9 %collective-permute-done.58 = bf16[144,384]{1,0:T(8,128)(2,1)S(1)} collective-permute-done((bf16[144,384]{1,0:T(8,128)(2,1)S(1)}, bf16[144,384]{1,0:T(8,128)(2,1)S(1)}, u32[]{:S(2)}, u32[]{:S(2)}) %collective-permute-start.58) | collective-permute-done | bytes 110624 | tf_op jit(solution)/shard_map/ppermute | solution.py:408
  448.4 8.5 %collective-permute-done.70 = bf16[4,160,384]{2,1,0:T(8,128)(2,1)S(1)} collective-permute-done((bf16[4,160,384]{2,1,0:T(8,128)(2,1)S(1)}, bf16[4,160,384]{2,1,0:T(8,128)(2,1)S(1)}, u32[]{:S(2)}, u32[]{:S(2)}) %collective-permute-start.70) | collective-permute-done | bytes 491552 | tf_op jit(solution)/shard_map/ppermute | solution.py:408
  484.5 14.2 %collective-permute-done.80 = bf16[192,384]{1,0:T(8,128)(2,1)S(1)} collective-permute-done((bf16[192,384]{1,0:T(8,128)(2,1)S(1)}, bf16[192,384]{1,0:T(8,128)(2,1)S(1)}, u32[]{:S(2)}, u32[]{:S(2)}) %collective-permute-start.80) | collective-permute-done | bytes 147488 | tf_op jit(solution)/shard_map/ppermute | solution.py:408
  (510 shorter events, 245.0 us)
Async XLA Ops:
  0.7 83.0 %collective-permute-start = (s32[4]{0:T(128)}, s32[4]{0:T(128)S(1)}, u32[]{:S(2)}, u32[]{:S(2)}) collective-permute-start(s32[4]{0:T(128)} %param.31), channel_id=1, source_target_pairs={{0,16},{16,0},{1,17},{17,1},{2,18},{18,2},{3,19},{19,3},{4,20},{20... | collective-permute-start | bytes 56 | tf_op jit(solution)/shard_map/ppermute | solution.py:417
  13.1 29.0 %collective-permute-start.21 = (bf16[144,384]{1,0:T(8,128)(2,1)S(1)}, bf16[144,384]{1,0:T(8,128)(2,1)S(1)}, u32[]{:S(2)}, u32[]{:S(2)}) collective-permute-start(bf16[144,384]{1,0:T(8,128)(2,1)S(1)} %constant_dynamic-update-slice_fusion.22), channel_id=1, source_target_pairs={{0,12},{1,13},{2,14},{3,15},{4,8},{5,9},{6,10},{7,11},{8,4},{9,5},... | collective-permute-start | bytes 331784 | tf_op jit(solution)/shard_map/ppermute | solution.py:408
  42.0 37.9 %collective-permute-start.29 = (bf16[192,384]{1,0:T(8,128)(2,1)S(1)}, bf16[192,384]{1,0:T(8,128)(2,1)S(1)}, u32[]{:S(2)}, u32[]{:S(2)}) collective-permute-start(bf16[192,384]{1,0:T(8,128)(2,1)S(1)} %constant_dynamic-update-slice_fusion.33), channel_id=1, source_target_pairs={{0,12},{1,13},{2,14},{3,15},{4,8},{5,9},{6,10},{7,11},{8,4},{9,5},... | collective-permute-start | bytes 442376 | tf_op jit(solution)/shard_map/ppermute | solution.py:408
  49.6 31.9 %collective-permute-start.28 = (bf16[192,384]{1,0:T(8,128)(2,1)S(1)}, bf16[192,384]{1,0:T(8,128)(2,1)S(1)}, u32[]{:S(2)}, u32[]{:S(2)}) collective-permute-start(bf16[192,384]{1,0:T(8,128)(2,1)S(1)} %constant_dynamic-update-slice_fusion.33), channel_id=1, source_target_pairs={{0,8},{1,9},{2,10},{3,11},{4,12},{5,13},{6,14},{7,15},{8,0},{9,1},... | collective-permute-start | bytes 442376 | tf_op jit(solution)/shard_map/ppermute | solution.py:408
  105.4 39.7 %collective-permute-start.23 = (bf16[8,144,384]{2,1,0:T(8,128)(2,1)S(1)}, bf16[8,144,384]{2,1,0:T(8,128)(2,1)S(1)}, u32[]{:S(2)}, u32[]{:S(2)}) collective-permute-start(bf16[8,144,384]{2,1,0:T(8,128)(2,1)S(1)} %constant_dynamic-update-slice_fusion.28.refs_12_.refs_10_), channel_id=1, source_target_pairs={{0,2},{1,3},{2,0},{3,1},{4,6},{5,7},{6,4},{7,5},{8,10},{9,11},{10,... | collective-permute-start | bytes 2654216 | tf_op jit(solution)/shard_map/ppermute | solution.py:408
  109.9 36.2 %collective-permute-start.16 = (bf16[8,160,384]{2,1,0:T(8,128)(2,1)S(1)}, bf16[8,160,384]{2,1,0:T(8,128)(2,1)S(1)}, u32[]{:S(2)}, u32[]{:S(2)}) collective-permute-start(bf16[8,160,384]{2,1,0:T(8,128)(2,1)S(1)} %constant_dynamic-update-slice_fusion.17.refs_4_.refs_5_), channel_id=1, source_target_pairs={{0,1},{1,0},{2,3},{3,2},{4,5},{5,4},{6,7},{7,6},{8,9},{9,8},{10,11... | collective-permute-start | bytes 2949128 | tf_op jit(solution)/shard_map/ppermute | solution.py:408
  112.1 50.4 %collective-permute-start.31 = (bf16[8,192,384]{2,1,0:T(8,128)(2,1)S(1)}, bf16[8,192,384]{2,1,0:T(8,128)(2,1)S(1)}, u32[]{:S(2)}, u32[]{:S(2)}) collective-permute-start(bf16[8,192,384]{2,1,0:T(8,128)(2,1)S(1)} %constant_dynamic-update-slice_fusion.41.refs_3_.refs_6_), channel_id=1, source_target_pairs={{0,16},{1,17},{2,18},{3,19},{4,20},{5,21},{6,22},{7,23},{8,24},{9,... | collective-permute-start | bytes 3538952 | tf_op jit(solution)/shard_map/ppermute | solution.py:408
  126.2 38.3 %collective-permute-start.40 = (bf16[8,192,384]{2,1,0:T(8,128)(2,1)}, bf16[8,192,384]{2,1,0:T(8,128)(2,1)}, u32[]{:S(2)}, u32[]{:S(2)}) collective-permute-start(bf16[8,192,384]{2,1,0:T(8,128)(2,1)} %constant_dynamic-update-slice_fusion.46.refs_8_), channel_id=1, source_target_pairs={{0,2},{1,3},{2,0},{3,1},{4,6},{5,7},{6,4},{7,5},{8,10},{9,11},{10,... | collective-permute-start | bytes 3538952 | tf_op jit(solution)/shard_map/ppermute | solution.py:408
  128.7 32.9 %collective-permute-start.15 = (bf16[8,160,384]{2,1,0:T(8,128)(2,1)S(1)}, bf16[8,160,384]{2,1,0:T(8,128)(2,1)S(1)}, u32[]{:S(2)}, u32[]{:S(2)}) collective-permute-start(bf16[8,160,384]{2,1,0:T(8,128)(2,1)S(1)} %constant_dynamic-update-slice_fusion.17.refs_4_.refs_5_), channel_id=1, source_target_pairs={{0,16},{1,17},{2,18},{3,19},{4,20},{5,21},{6,22},{7,23},{8,24},{9,... | collective-permute-start | bytes 2949128 | tf_op jit(solution)/shard_map/ppermute | solution.py:408
  162.5 54.9 %collective-permute-start.32 = (bf16[8,192,384]{2,1,0:T(8,128)(2,1)S(1)}, bf16[8,192,384]{2,1,0:T(8,128)(2,1)S(1)}, u32[]{:S(2)}, u32[]{:S(2)}) collective-permute-start(bf16[8,192,384]{2,1,0:T(8,128)(2,1)S(1)} %constant_dynamic-update-slice_fusion.41.refs_3_.refs_6_), channel_id=1, source_target_pairs={{0,1},{1,0},{2,3},{3,2},{4,5},{5,4},{6,7},{7,6},{8,9},{9,8},{10,11... | collective-permute-start | bytes 3538952 | tf_op jit(solution)/shard_map/ppermute | solution.py:408
  164.5 52.9 %collective-permute-start.33 = (bf16[8,192,384]{2,1,0:T(8,128)(2,1)S(1)}, bf16[8,192,384]{2,1,0:T(8,128)(2,1)}, u32[]{:S(2)}, u32[]{:S(2)}) collective-permute-start(bf16[8,192,384]{2,1,0:T(8,128)(2,1)S(1)} %collective-permute-done.31.refs_4_.refs_7_), channel_id=1, source_target_pairs={{0,1},{1,0},{2,3},{3,2},{4,5},{5,4},{6,7},{7,6},{8,9},{9,8},{10,11... | collective-permute-start | bytes 3538952 | tf_op jit(solution)/shard_map/ppermute | solution.py:408
  165.4 58.7 %collective-permute-start.41 = (bf16[8,192,384]{2,1,0:T(8,128)(2,1)}, bf16[8,192,384]{2,1,0:T(8,128)(2,1)}, u32[]{:S(2)}, u32[]{:S(2)}) collective-permute-start(bf16[8,192,384]{2,1,0:T(8,128)(2,1)} %constant_dynamic-update-slice_fusion.46.refs_8_), channel_id=1, source_target_pairs={{0,1},{1,0},{2,3},{3,2},{4,5},{5,4},{6,7},{7,6},{8,9},{9,8},{10,11... | collective-permute-start | bytes 3538952 | tf_op jit(solution)/shard_map/ppermute | solution.py:408
  166.0 58.2 %collective-permute-start.42 = (bf16[8,192,384]{2,1,0:T(8,128)(2,1)}, bf16[8,192,384]{2,1,0:T(8,128)(2,1)}, u32[]{:S(2)}, u32[]{:S(2)}) collective-permute-start(bf16[8,192,384]{2,1,0:T(8,128)(2,1)} %collective-permute-done.40.refs_9_), channel_id=1, source_target_pairs={{0,1},{1,0},{2,3},{3,2},{4,5},{5,4},{6,7},{7,6},{8,9},{9,8},{10,11... | collective-permute-start | bytes 3538952 | tf_op jit(solution)/shard_map/ppermute | solution.py:408
  167.8 56.3 %collective-permute-start.34 = (bf16[192,768]{1,0:T(8,128)(2,1)}, bf16[192,768]{1,0:T(8,128)(2,1)}, u32[]{:S(2)}, u32[]{:S(2)}) collective-permute-start(bf16[192,768]{1,0:T(8,128)(2,1)} %bitcast.21), channel_id=1, source_target_pairs={{0,16},{16,0},{1,17},{17,1},{2,18},{18,2},{3,19},{19,3},{4,20},{20... | collective-permute-start | bytes 884744 | tf_op jit(solution)/shard_map/ppermute | solution.py:417
  303.0 35.6 %collective-permute-start.46 = (bf16[8,144,384]{2,1,0:T(8,128)(2,1)}, bf16[8,144,384]{2,1,0:T(8,128)(2,1)}, u32[]{:S(2)}, u32[]{:S(2)}) collective-permute-start(bf16[8,144,384]{2,1,0:T(8,128)(2,1)} %get-tuple-element.107), channel_id=1, source_target_pairs={{0,1},{1,0},{2,3},{3,2},{4,5},{5,4},{6,7},{7,6},{8,9},{9,8},{10,11... | collective-permute-start | bytes 2654216 | tf_op jit(solution)/shard_map/ppermute | solution.py:408
  345.6 38.0 %collective-permute-start.55 = (bf16[8,144,384]{2,1,0:T(8,128)(2,1)S(1)}, bf16[8,144,384]{2,1,0:T(8,128)(2,1)S(1)}, u32[]{:S(2)}, u32[]{:S(2)}) collective-permute-start(bf16[8,144,384]{2,1,0:T(8,128)(2,1)S(1)} %add_convert_fusion.3), channel_id=1, source_target_pairs={{0,2},{1,3},{2,0},{3,1},{4,6},{5,7},{6,4},{7,5},{8,10},{9,11},{10,... | collective-permute-start | bytes 2654216 | tf_op jit(solution)/shard_map/ppermute | solution.py:408
  347.8 37.6 %collective-permute-start.67 = (bf16[8,160,384]{2,1,0:T(8,128)(2,1)S(1)}, bf16[8,160,384]{2,1,0:T(8,128)(2,1)S(1)}, u32[]{:S(2)}, u32[]{:S(2)}) collective-permute-start(bf16[8,160,384]{2,1,0:T(8,128)(2,1)S(1)} %copy-done.60), channel_id=1, source_target_pairs={{0,1},{1,0},{2,3},{3,2},{4,5},{5,4},{6,7},{7,6},{8,9},{9,8},{10,11... | collective-permute-start | bytes 2949128 | tf_op jit(solution)/shard_map/ppermute | solution.py:408
  347.9 38.1 %collective-permute-start.69 = (bf16[8,160,384]{2,1,0:T(8,128)(2,1)S(1)}, bf16[8,160,384]{2,1,0:T(8,128)(2,1)S(1)}, u32[]{:S(2)}, u32[]{:S(2)}) collective-permute-start(bf16[8,160,384]{2,1,0:T(8,128)(2,1)S(1)} %add_convert_fusion.2), channel_id=1, source_target_pairs={{0,16},{1,17},{2,18},{3,19},{4,20},{5,21},{6,22},{7,23},{8,24},{9,... | collective-permute-start | bytes 2949128 | tf_op jit(solution)/shard_map/ppermute | solution.py:408
  365.1 79.1 %collective-permute-start.75 = (bf16[8,192,384]{2,1,0:T(8,128)(2,1)S(1)}, bf16[8,192,384]{2,1,0:T(8,128)(2,1)S(1)}, u32[]{:S(2)}, u32[]{:S(2)}) collective-permute-start(bf16[8,192,384]{2,1,0:T(8,128)(2,1)S(1)} %copy-done.58), channel_id=1, source_target_pairs={{0,1},{1,0},{2,3},{3,2},{4,5},{5,4},{6,7},{7,6},{8,9},{9,8},{10,11... | collective-permute-start | bytes 3538952 | tf_op jit(solution)/shard_map/ppermute | solution.py:408
  366.6 77.7 %collective-permute-start.77 = (bf16[8,192,384]{2,1,0:T(8,128)(2,1)S(1)}, bf16[8,192,384]{2,1,0:T(8,128)(2,1)S(1)}, u32[]{:S(2)}, u32[]{:S(2)}) collective-permute-start(bf16[8,192,384]{2,1,0:T(8,128)(2,1)S(1)} %add_convert_fusion.1), channel_id=1, source_target_pairs={{0,16},{1,17},{2,18},{3,19},{4,20},{5,21},{6,22},{7,23},{8,24},{9,... | collective-permute-start | bytes 3538952 | tf_op jit(solution)/shard_map/ppermute | solution.py:408
  385.5 30.9 %collective-permute-start.56 = (bf16[4,144,384]{2,1,0:T(8,128)(2,1)S(1)}, bf16[4,144,384]{2,1,0:T(8,128)(2,1)S(1)}, u32[]{:S(2)}, u32[]{:S(2)}) collective-permute-start(bf16[4,144,384]{2,1,0:T(8,128)(2,1)S(1)} %slice.1085), channel_id=1, source_target_pairs={{0,16},{1,17},{2,18},{3,19},{4,20},{5,21},{6,22},{7,23},{8,24},{9,... | collective-permute-start | bytes 1327112 | tf_op jit(solution)/shard_map/ppermute | solution.py:408
  417.6 28.8 %collective-permute-start.85 = (bf16[8,192,384]{2,1,0:T(8,128)(2,1)S(1)}, bf16[8,192,384]{2,1,0:T(8,128)(2,1)S(1)}, u32[]{:S(2)}, u32[]{:S(2)}) collective-permute-start(bf16[8,192,384]{2,1,0:T(8,128)(2,1)S(1)} %add_convert_fusion), channel_id=1, source_target_pairs={{0,2},{1,3},{2,0},{3,1},{4,6},{5,7},{6,4},{7,5},{8,10},{9,11},{10,... | collective-permute-start | bytes 3538952 | tf_op jit(solution)/shard_map/ppermute | solution.py:408
  444.8 29.7 %collective-permute-start.78 = (bf16[4,192,384]{2,1,0:T(8,128)(2,1)S(1)}, bf16[4,192,384]{2,1,0:T(8,128)(2,1)S(1)}, u32[]{:S(2)}, u32[]{:S(2)}) collective-permute-start(bf16[4,192,384]{2,1,0:T(8,128)(2,1)S(1)} %slice.1083), channel_id=1, source_target_pairs={{0,2},{1,3},{2,0},{3,1},{4,6},{5,7},{6,4},{7,5},{8,10},{9,11},{10,... | collective-permute-start | bytes 1769480 | tf_op jit(solution)/shard_map/ppermute | solution.py:408
  446.8 31.4 %collective-permute-start.86 = (bf16[4,192,384]{2,1,0:T(8,128)(2,1)S(1)}, bf16[4,192,384]{2,1,0:T(8,128)(2,1)S(1)}, u32[]{:S(2)}, u32[]{:S(2)}) collective-permute-start(bf16[4,192,384]{2,1,0:T(8,128)(2,1)S(1)} %slice.1082), channel_id=1, source_target_pairs={{0,16},{1,17},{2,18},{3,19},{4,20},{5,21},{6,22},{7,23},{8,24},{9,... | collective-permute-start | bytes 1769480 | tf_op jit(solution)/shard_map/ppermute | solution.py:408
  (155 other events, 1840.7 us)
